TPU v7x, 128 devices: a whole 4x4x4 slice. The times are simulated.
128 devices in a mesh: batch: 32 (over z, x, core), hidden: 4 (over y).
Axes of the slice: x: 4, y: 4, z: 4, core: 2. Of those that a mesh axis runs over, the one named last changes fastest.
Arguments:
- tables: float32 [26, 131072, 16], P(None, ('batch', 'hidden')), may hold values from -6 to 6
- dense: float32 [16384, 13], P('batch'), may hold values from -6 to 6
- dense_weight: float32 [13, 96], replicated, may hold values from -1.75 to 1.75
- expert_in: float32 [512, 8, 256], P(None, None, 'hidden'), may hold values from -0.25 to 0.25
- expert_out: float32 [8, 256, 128], P(None, 'hidden'), may hold values from -0.375 to 0.375
- gate_weight: float32 [2, 512, 8], replicated, may hold values from -0.125 to 0.125
- tower_weight: float32 [2, 128, 64], replicated, may hold values from -0.5 to 0.5
- head_weight: float32 [2, 64], replicated, may hold values from -0.75 to 0.75
- slots: int32 [16384, 26], P('batch'), may hold values from 0 to 4095, as said below
- requests: int32 [32, 128, 32], P('batch'), may hold values from 0 to 26623
- pred_cot: float32 [16384, 2], P(('batch', 'hidden')), may hold values from -6 to 6
Outputs:
- predictions: float32 [16384, 2], P(('batch', 'hidden'))
- dense_grad: float32 [16384, 13], P('batch')
- table_grad: float32 [26, 131072, 16], P(None, ('batch', 'hidden'))
- dense_weight_grad: float32 [13, 96], replicated
- expert_in_grad: float32 [512, 8, 256], P(None, None, 'hidden')
- expert_out_grad: float32 [8, 256, 128], P(None, 'hidden')
- gate_grad: float32 [2, 512, 8], replicated
- tower_grad: float32 [2, 128, 64], replicated
- head_grad: float32 [2, 64], replicated
Inputs may be any that keep to these rules, and one draw needn't show every extreme that they name: slots[e, t] = o * 32 + j names slot j of owner o in the fetch list of the example's group; in every group some owner has all 32 slots named, and every owner is named. requests[g, o, j] = v names row o * 1024 + (v mod 1024) of table floor(v / 1024).
All inputs are finite; a program needn't handle non-finite values.
Results may differ from a plain program's by a relative error of at most 0.0003.
Values sent between devices are 32-bit elements; how exact they have to be, the bound alone decides.
A program may use at most 64 MiB of HBM per device.

v0:
```python
import jax
import jax.numpy as jnp
from jax import lax
from jax.experimental import pallas as pl
from jax.experimental.pallas import tpu as pltpu
from jax.sharding import PartitionSpec as P

f32 = jnp.float32
bf16 = jnp.bfloat16
MESH = pl.DeviceIdType.MESH
VMEM = pl.BlockSpec(memory_space=pltpu.VMEM)
LIMIT = 56 * 2**20

TABLES, ROWS, ENTRY = 26, 1024, 16
BATCH, HIDDEN = 32, 4
DEVICES = BATCH * HIDDEN
EXPERTS, UNITS, OUT, WIDTH = 8, 64, 128, 512
TASKS, TOWER, DENSE, PROJ = 2, 64, 13, 96
EXAMPLES = 512
EMBED = TABLES * ENTRY

IN_PARTS = ((0, 3), (3, 6), (6, 8))
IN_ROWS = 2048
OUT_AT, GATE_AT, TOWER_AT, HEAD_AT = 0, 512, 576, 704
REST_ROWS, REST_PIECE = 768, 24


def split(value):
    high = value.astype(bf16)
    return high, (value - high.astype(f32)).astype(bf16)


def dot_nn(a, b):
    return lax.dot_general(a, b, (((1,), (0,)), ((), ())), preferred_element_type=f32)


def dot_nt(a, b):
    return lax.dot_general(a, b, (((1,), (1,)), ((), ())), preferred_element_type=f32)


def dot_tn(a, b):
    return lax.dot_general(a, b, (((0,), (0,)), ((), ())), preferred_element_type=f32)


def dot3_tn(a, b):
    (ah, al), (bh, bl) = a, b
    return dot_tn(ah, bh) + dot_tn(al, bh) + dot_tn(ah, bl)


def dot3_nn(a, b):
    (ah, al), (bh, bl) = a, b
    return dot_nn(jnp.concatenate([ah, al, ah], 1), jnp.concatenate([bh, bh, bl], 0))


def dot3_nt(a, b):
    (ah, al), (bh, bl) = a, b
    return dot_nt(jnp.concatenate([ah, al, ah], 1), jnp.concatenate([bh, bh, bl], 1))


def sigmoid(value):
    return 0.5 * jnp.tanh(0.5 * value) + 0.5


def silu_both(value):
    sigma = sigmoid(value)
    result = value * sigma
    return result, sigma + result * (1.0 - sigma)


def iota(shape, axis):
    return lax.broadcasted_iota(jnp.int32, shape, axis)


def hops(offset):
    return min(offset, 4 - offset)


PLANE = sorted(
    ((dz, dx, dc) for dz in range(4) for dx in range(4) for dc in range(2) if dz or dx or dc),
    key=lambda d: -(2 * hops(d[0]) + 2 * hops(d[1]) + d[2]),
)
EVERYWHERE = sorted(
    ((dz, dx, dc, dy) for dz in range(4) for dx in range(4) for dc in range(2) for dy in range(4) if dz or dx or dc or dy),
    key=lambda d: -(2 * hops(d[0]) + 2 * hops(d[1]) + d[2] + 2 * hops(d[3])),
)
CHIPS = [(dz, dx) for dz, dx, dc in PLANE if not dc and (dz or dx)]


def target(b, h):
    return {"batch": b, "hidden": h}


def remote(src, dst, send, recv, b, h):
    return pltpu.make_async_remote_copy(src, dst, send, recv, device_id=target(b, h), device_id_type=MESH)


def bulk_wait(ref, sem):
    pltpu.make_async_copy(ref, ref, sem).wait()


def ids_by_query(received):
    turned = jnp.concatenate([received] * 4, 0).T
    lane = iota((8, 128), 1) // 32
    out = jnp.zeros((8, 128), jnp.int32)
    for q in range(4):
        out = jnp.where(lane == q, turned[q * 8 : q * 8 + 8, :], out)
    return out


def hot_of(code, count):
    rows = iota((count, code.shape[1]), 0).astype(jnp.int16)
    return jnp.where(rows == code.astype(jnp.int16), bf16(1.0), bf16(0.0))


def model_kernel(
    req_in, tab_in, win, wout, cot_in, slots_in, dense_in, dense_weight_in, gate_weight_in, tower_weight_in, head_in,
    pred_out, dense_grad_out, table_out, in_total, rest_total, weight_grad_out, head_grad_out,
    req, tab, cot, slots, dense, dense_weight, gate_weight, tower_weight, head,
    id_turned, id_send, id_recv, ids, row_send, rows, tab_split, win_all, wout_all, cot_all,
    wh, wl, oh, ol, gate_h, gate_l, tower_h, tower_l, dense_h, dense_l, lists, feat_h, feat_l,
    dense_pad, weight_pad, head_pad,
    inner_h, inner_l, slope, ig_h, ig_l, eo, eslope, ep_h, ep_l, gates, gate_slope, mixed, mixed_grad, pred,
    towers, pre_grads, scores, lgh, lgl, fg, slot_sum,
    in_sums, rest_sums, in_swap, rest_swap, in_pieces, rest_pieces,
    message, got, weight_part, weight_swap, weight_got, weight_total, hot_rows, hot_slots,
    local_sem, y_ssem, y_rsem, p_ssem, p_rsem, c_ssem, c_rsem, wo_ssem, wo_rsem, woc_ssem, woc_rsem, cot_ssem, cot_rsem,
    id_ssem, id_rsem, row_ssem, row_rsem, slot_ssem, slot_rsem, weight_ssem, weight_rsem, weight_send, weight_recv,
    swap_ssem, swap_rsem, piece_ssem, piece_rsem, full_ssem, full_rsem, last_ssem, last_rsem,
):
    b, h = lax.axis_index("batch"), lax.axis_index("hidden")
    core, x, z, chip = lax.rem(b, 2), lax.rem(b // 2, 4), b // 8, b // 2
    me = b * HIDDEN + h
    sibling = b + 1 - 2 * core
    zs = [lax.rem(z + d, 4) * 8 for d in range(4)]
    xs = [lax.rem(x + d, 4) * 2 for d in range(4)]
    cores = [core, 1 - core]
    hs = [lax.rem(h + d, HIDDEN) for d in range(HIDDEN)]
    chips = [(zs[dz] + xs[dx]) // 2 for dz, dx in CHIPS]
    plane = [zs[dz] + xs[dx] + cores[dc] for dz, dx, dc in PLANE]
    order = (1, 3, 2)
    block = pl.when(core >= 0)

    def bring(source, home, i):
        copy = pltpu.make_async_copy(source, home, local_sem.at[i])
        copy.start()
        return copy

    def units_of(s, e):
        return pl.ds(pl.multiple_of(s * 512 + e * UNITS, UNITS), UNITS)

    def block_of(s):
        return pl.ds(pl.multiple_of(s * 512, 512), 512)

    req_copy = bring(req_in, req, 0)
    barrier = pltpu.get_barrier_semaphore()
    for other in plane:
        pl.semaphore_signal(barrier, inc=1, device_id=target(other, h), device_id_type=MESH)
    for i in (2, 1, 3):
        pl.semaphore_signal(barrier, inc=1, device_id=target(b, hs[i]), device_id_type=MESH)
    tab_copy = bring(tab_in, tab, 1)
    win_copy = bring(win, win_all.at[h], 2)
    wout_copy = bring(wout, wout_all.at[h], 3)
    small = ((cot_in, cot), (slots_in, slots), (dense_in, dense), (dense_weight_in, dense_weight),
             (gate_weight_in, gate_weight), (tower_weight_in, tower_weight), (head_in, head))
    small_copies = [bring(source, home, 4 + i) for i, (source, home) in enumerate(small)]
    req_copy.wait()
    id_turned[...] = jnp.concatenate([req[...]] * 4, 0).T
    id_send[...] = id_turned[pl.ds(h, BATCH, stride=HIDDEN), :]
    pl.semaphore_wait(barrier, BATCH - 1 + HIDDEN - 1)

    for other in plane:
        remote(id_send.at[pl.ds(other, 1)], id_recv.at[pl.ds(b, 1)], id_ssem, id_rsem, other, h).start()
    spots = (
        pl.ds(pl.multiple_of(core * 128 + x * 32, 32), 32),
        pl.ds(pl.multiple_of(256 + core * 128 + z * 32, 32), 32),
    )
    spans = (pl.ds(pl.multiple_of(core * 128, 128), 128), pl.ds(pl.multiple_of(256 + core * 128, 128), 128))
    half = pl.ds(pl.multiple_of(core * 256, 256), 256)
    source_of = [lax.rem(h - i + HIDDEN, HIDDEN) for i in range(HIDDEN)]
    for i in order:
        for spot in spots:
            remote(win.at[spot], win_all.at[h, spot], y_ssem, y_rsem.at[i - 1], b, hs[i]).start()

    def spread(i):
        source = source_of[i]
        bulk_wait(win_all.at[source, pl.ds(0, 64)], y_rsem.at[i - 1])
        for j in (2, 1, 3):
            for spot, other in ((spots[0], z * 8 + xs[j] + core), (spots[1], zs[j] + x * 2 + core)):
                piece = win_all.at[source, spot]
                remote(piece, piece, p_ssem, p_rsem.at[i - 1], other, h).start()

    def to_core(i):
        source = source_of[i]
        bulk_wait(win_all.at[source, pl.ds(0, 192)], p_rsem.at[i - 1])
        for span in spans:
            piece = win_all.at[source, span]
            remote(piece, piece, c_ssem, c_rsem.at[i - 1], sibling, h).start()

    def out_to_core(i):
        bulk_wait(wout_all.at[source_of[i], half], wo_rsem.at[i - 1])
        piece = wout_all.at[source_of[i], half]
        remote(piece, piece, woc_ssem, woc_rsem, sibling, h).start()

    tab_copy.wait()

    @block
    def _():
        high, low = split(tab[...])
        tab_split[0:EMBED, :] = high
        tab_split[EMBED : 2 * EMBED, :] = low

    id_recv[pl.ds(b, 1), :] = id_send[pl.ds(b, 1), :]
    bulk_wait(id_recv.at[pl.ds(0, BATCH - 1)], id_rsem)

    @block
    def _():
        found = ids_by_query(id_recv[...])
        ids[...] = found
        table, row = found // ROWS, lax.rem(found, ROWS)
        entries = []
        for pair in range(4):
            hot = jnp.concatenate([hot_of(row[j : j + 1, :], ROWS) for j in (2 * pair, 2 * pair + 1)], 1)
            value = dot_nn(tab_split[...], hot)
            for part in range(2):
                wanted = table[2 * pair + part : 2 * pair + part + 1, :]
                entry = jnp.zeros((ENTRY, 128), f32)
                for t in range(TABLES):
                    high = value[t * ENTRY : (t + 1) * ENTRY, part * 128 : part * 128 + 128]
                    low = value[EMBED + t * ENTRY : EMBED + (t + 1) * ENTRY, part * 128 : part * 128 + 128]
                    entry = jnp.where(wanted == t, high + low, entry)
                entries.append(entry)
        turned = jnp.concatenate(entries, 0).T
        for q in range(4):
            row_send[pl.ds(q, BATCH, stride=4), :] = turned[q * 32 : q * 32 + 32, :]

    mine = pl.ds(me * 4, 4)
    for dz, dx, dc, dy in EVERYWHERE:
        group = zs[dz] + xs[dx] + cores[dc]
        remote(row_send.at[pl.ds(group * 4, 4)], rows.at[mine], row_ssem, row_rsem, group, hs[dy]).start()
    rows[mine, :] = row_send[pl.ds(b * 4, 4), :]
    for i in order:
        spread(i)
    for copy in small_copies:
        copy.wait()
    wout_copy.wait()
    for i in order:
        remote(cot, cot_all.at[h], cot_ssem, cot_rsem, b, hs[i]).start()
        piece = wout_all.at[h, half]
        remote(piece, piece, wo_ssem, wo_rsem.at[i - 1], b, hs[i]).start()
    win_copy.wait()

    @block
    def _():
        cot_all[pl.ds(h, 1)] = cot[...].reshape(1, TASKS, 128)
        dense_pad[...] = jnp.zeros_like(dense_pad)
        dense_pad[0:DENSE, :] = dense[...]
        weight_pad[...] = jnp.zeros_like(weight_pad)
        weight_pad[0:DENSE, 0:PROJ] = dense_weight[...]
        head_pad[...] = jnp.zeros_like(head_pad)
        head_pad[0:TASKS, 0:TOWER] = head[...]
        dense_h[...], dense_l[...] = split(dense_pad[...])
        projected = dot3_nn(split(weight_pad[...].T), (dense_h[...], dense_l[...]))
        feat_h[EMBED:WIDTH, :], feat_l[EMBED:WIDTH, :] = split(projected[0:PROJ, :])
        tower_h[...], tower_l[...] = split(tower_weight[...])
        gate_h[...], gate_l[...] = split(gate_weight[...])
        wh[block_of(h), :], wl[block_of(h), :] = split(win_all[h])

    @block
    def _():
        row = lax.rem(ids[...], ROWS)
        for j in range(8):
            hot_rows[:, j * 128 : (j + 1) * 128] = hot_of(row[j : j + 1, :], ROWS)

    @block
    def _():
        for t in range(TABLES):
            slot = slots[t : t + 1, :]
            owner = slot // 32
            code = jnp.where(lax.rem(owner, HIDDEN) == h, lax.rem(slot, 32) // 8 * 32 + owner // HIDDEN, -1)
            hot_slots[:, t * EXAMPLES : (t + 1) * EXAMPLES] = hot_of(code, 128)

    bulk_wait(rows.at[pl.ds(0, (DEVICES - 1) * 4)], row_rsem)

    def gather(first, last):
        for t in range(first, last):
            slot = slots[t : t + 1, :]
            low = lax.rem(slot, 8)
            value = dot_nn(lists[...], hot_of(lax.rem(slot, 32) // 8 * 128 + slot // 32, 512))
            high_sum = jnp.zeros((ENTRY, EXAMPLES), f32)
            low_sum = jnp.zeros((ENTRY, EXAMPLES), f32)
            for j in range(8):
                high_sum = jnp.where(low == j, value[j * 16 : j * 16 + 16, :], high_sum)
                low_sum = jnp.where(low == j, value[128 + j * 16 : 128 + j * 16 + 16, :], low_sum)
            feat_h[t * ENTRY : (t + 1) * ENTRY, :] = high_sum.astype(bf16)
            feat_l[t * ENTRY : (t + 1) * ENTRY, :] = low_sum.astype(bf16)

    @block
    def _():
        for q in range(4):
            at = slice(q * 128, q * 128 + 128)
            lists[0:128, at], lists[128:256, at] = split(rows[pl.ds(q, DEVICES, stride=4), :].T)
        gather(0, 13)

    to_core(1)
    block(lambda: gather(13, TABLES))

    def first_layer(s):
        at = block_of(s)
        inner, slope[at, :] = silu_both(dot3_nn((wh[at, :], wl[at, :]), (feat_h[...], feat_l[...])))
        inner_h[at, :], inner_l[at, :] = split(inner)

    def next_layer(*which):
        for i in which:
            bulk_wait(win_all.at[source_of[i], pl.ds(0, 256)], c_rsem.at[i - 1])

        @block
        def _():
            for i in which:
                s = source_of[i]
                wh[block_of(s), :], wl[block_of(s), :] = split(win_all[s])
                first_layer(s)

    @block
    def _():
        first_layer(h)
        logits = dot3_nn((gate_h[...], gate_l[...]), (feat_h[...], feat_l[...]))
        for k in range(TASKS):
            part = logits[k * 8 : k * 8 + 8, :]
            raised = jnp.exp(part - jnp.max(part, axis=0, keepdims=True))
            gates[k * 8 : k * 8 + 8, :] = raised / jnp.sum(raised, axis=0, keepdims=True)

    to_core(3)
    next_layer(1)
    to_core(2)
    next_layer(3)
    for i in order:
        out_to_core(i)
    next_layer(2)
    bulk_wait(wout_all.at[pl.ds(0, 3), pl.ds(0, 256)], woc_rsem)
    bulk_wait(cot_all.at[pl.ds(0, 3)], cot_rsem)

    def of_expert(refs, e):
        return tuple(
            jnp.concatenate([ref[s * 512 + e * UNITS : s * 512 + (e + 1) * UNITS, :] for s in range(HIDDEN)], 0)
            for ref in refs
        )

    @block
    def _():
        mixed[...] = jnp.zeros_like(mixed)
        for s in range(HIDDEN):
            at = slice(s * 512, s * 512 + 512)
            oh[at, :], ol[at, :] = split(wout_all[s])
        for e in range(EXPERTS):
            outputs, eslope[e] = silu_both(dot3_tn(of_expert((oh, ol), e), of_expert((inner_h, inner_l), e)))
            eo[e] = outputs
            for k in range(TASKS):
                mixed[k] = mixed[k] + gates[k * 8 + e : k * 8 + e + 1, :] * outputs

    @block
    def _():
        head_turned = head_pad[...].T
        scores[...] = jnp.zeros_like(scores)
        for k in range(TASKS):
            at = slice(k * TOWER, (k + 1) * TOWER)
            value, tower_slope = silu_both(dot3_nn((tower_h[at, :], tower_l[at, :]), split(mixed[k])))
            column = jnp.broadcast_to(head_turned[0:TOWER, k : k + 1], (TOWER, EXAMPLES))
            predicted = sigmoid(jnp.sum(value * column, axis=0, keepdims=True))
            pred[k : k + 1, :] = predicted
            cotangent = jnp.concatenate([cot_all[i, k : k + 1, :] for i in range(HIDDEN)], 1)
            score = cotangent * predicted * (1.0 - predicted)
            scores[k : k + 1, :] = score
            towers[at, :] = value
            pre_grad = score * column * tower_slope
            pre_grads[at, :] = pre_grad
            mixed_grad[k] = dot3_tn((tower_h[at, :], tower_l[at, :]), split(pre_grad))

    def expert_grads(first, last):
        for e in range(first, last):
            outputs = eo[e]
            grad = jnp.zeros((OUT, EXAMPLES), f32)
            for k in range(TASKS):
                gate_slope[k * 8 + e : k * 8 + e + 1, :] = jnp.sum(mixed_grad[k] * outputs, axis=0, keepdims=True)
                grad = grad + gates[k * 8 + e : k * 8 + e + 1, :] * mixed_grad[k]
            out_split = split(grad * eslope[e])
            ep_h[e], ep_l[e] = out_split
            at = units_of(h, e)
            ig_h[at, :], ig_l[at, :] = split(dot3_nn((oh[at, :], ol[at, :]), out_split) * slope[at, :])

    def other_grads():
        for e in range(EXPERTS):
            places = [units_of(source_of[i], e) for i in order]
            side = tuple(jnp.concatenate([ref[at, :] for at in places], 0) for ref in (oh, ol))
            inner_grad = dot3_nn(side, (ep_h[e], ep_l[e]))
            for n, at in enumerate(places):
                ig_h[at, :], ig_l[at, :] = split(inner_grad[n * UNITS : (n + 1) * UNITS, :] * slope[at, :])

    def first_layer_grad(first, last):
        count = (last - first) * UNITS
        at = pl.ds(pl.multiple_of(h * 512 + first * UNITS, UNITS), count)
        ig, ig_low = ig_h[at, :], ig_l[at, :]
        in_grad = dot_nt(jnp.concatenate([ig, ig_low], 0), feat_h[...])
        in_grad = in_grad[0:count, :] + in_grad[count : 2 * count, :] + dot_nt(ig, feat_l[...])
        for q in range(4):
            start = 4 * first * UNITS + q * count
            in_sums[start : start + count, :] = in_grad[:, q * 128 : (q + 1) * 128]

    parts = []
    for first, last in IN_PARTS:
        start, size = 4 * first * UNITS, 4 * (last - first) * UNITS
        whole, halves = pl.ds(start, size), pl.ds(start // 2, size // 2)
        parts.append((in_sums.at[whole], in_swap.at[halves], in_pieces.at[halves], in_total.at[whole], size // 32))
    parts.append((rest_sums, rest_swap, rest_pieces, rest_total, REST_PIECE))

    def swap(n):
        sums, swapped, _, _, piece = parts[n]
        half_rows = 16 * piece
        theirs = sums.at[pl.ds(pl.multiple_of((1 - core) * half_rows, 8), half_rows)]
        remote(theirs, swapped, swap_ssem, swap_rsem.at[n], sibling, h).start()

    def send_pieces(n):
        sums, swapped, pieces, _, piece = parts[n]
        half_rows = 16 * piece
        bulk_wait(swapped, swap_rsem.at[n])
        swapped[...] += sums[pl.ds(pl.multiple_of(core * half_rows, 8), half_rows), :]
        own = pl.ds(pl.multiple_of(chip * piece, 8), piece)
        for other in chips:
            remote(
                swapped.at[pl.ds(pl.multiple_of(other * piece, 8), piece)], pieces.at[own],
                piece_ssem, piece_rsem.at[n], other * 2 + core, h,
            ).start()
        pieces[own, :] = swapped[own, :]

    def send_sums(n):
        _, _, pieces, total, piece = parts[n]
        half_rows = 16 * piece
        bulk_wait(pieces.at[pl.ds(0, 15 * piece)], piece_rsem.at[n])
        value = pieces[0:piece, :]
        for i in range(1, 16):
            value = value + pieces[i * piece : (i + 1) * piece, :]
        at = pl.ds(pl.multiple_of(core * half_rows + chip * piece, 8), piece)
        total[at, :] = value
        for other in chips:
            remote(total.at[at], total.at[at], full_ssem, full_rsem.at[n], other * 2 + core, h).start()

    def hand_on(n):
        _, _, _, total, piece = parts[n]
        bulk_wait(total.at[pl.ds(0, 15 * piece)], full_rsem.at[n])
        ours = total.at[pl.ds(pl.multiple_of(core * 16 * piece, 8), 16 * piece)]
        remote(ours, ours, last_ssem, last_rsem, sibling, h).start()

    for n, (first, last) in enumerate(IN_PARTS):

        @block
        def _():
            expert_grads(first, last)
            first_layer_grad(first, last)

        swap(n)
        if n:
            send_pieces(n - 1)

    @block
    def _():
        for k in range(TASKS):
            at = slice(k * TOWER, (k + 1) * TOWER)
            rest_sums[TOWER_AT + k * TOWER : TOWER_AT + (k + 1) * TOWER, :] = dot3_nt(
                split(pre_grads[at, :]), split(mixed[k])
            )
        head_rows = dot3_nt(split(scores[...]), split(towers[...]))
        rest_sums[HEAD_AT:REST_ROWS, :] = jnp.zeros((REST_ROWS - HEAD_AT, 128), f32)
        rest_sums[HEAD_AT : HEAD_AT + 1, :] = jnp.where(
            iota((1, 128), 1) < TOWER, head_rows[0:1, :], head_rows[1:2, :]
        )
        logit_grads = []
        for k in range(TASKS):
            gate, slopes = gates[k * 8 : k * 8 + 8, :], gate_slope[k * 8 : k * 8 + 8, :]
            logit_grads.append(gate * (slopes - jnp.sum(gate * slopes, axis=0, keepdims=True)))
        lgh[...], lgl[...] = split(jnp.concatenate(logit_grads, 0))
        gate_grad = dot3_nt((lgh[...], lgl[...]), (feat_h[...], feat_l[...]))
        for q in range(4):
            rest_sums[GATE_AT + q * 16 : GATE_AT + q * 16 + 16, :] = gate_grad[:, q * 128 : (q + 1) * 128]

    send_pieces(2)

    @block
    def _():
        for e in range(EXPERTS):
            at = units_of(h, e)
            rest_sums[OUT_AT + e * UNITS : OUT_AT + (e + 1) * UNITS, :] = dot3_nt(
                (inner_h[at, :], inner_l[at, :]), (ep_h[e], ep_l[e])
            )

    swap(3)

    def feature_grad(low, high):
        at = slice(low, high)
        fg[at, :] = dot3_tn((wh[:, at], wl[:, at]), (ig_h[...], ig_l[...])) + dot3_tn(
            (gate_h[:, at], gate_l[:, at]), (lgh[...], lgl[...])
        )

    def scatter(first, last):
        spreads = []
        for t in range(first, last):
            low = lax.rem(slots[t : t + 1, :], 8)
            high, rest = split(fg[t * ENTRY : (t + 1) * ENTRY, :])
            where = jnp.broadcast_to(low, (ENTRY, EXAMPLES)).astype(jnp.int16)
            nothing = jnp.zeros((ENTRY, EXAMPLES), bf16)
            spreads.append(
                jnp.concatenate([jnp.where(where == j, value, nothing) for value in (high, rest) for j in range(8)], 0)
            )
        return dot_nt(jnp.concatenate(spreads, 1), hot_slots[:, first * EXAMPLES : last * EXAMPLES])

    block(other_grads)
    send_pieces(3)
    block(lambda: feature_grad(256, WIDTH))
    send_sums(0)

    @block
    def _():
        projected_grad = split(jnp.concatenate([fg[EMBED:WIDTH, :], jnp.zeros((32, EXAMPLES), f32)], 0))
        weight_part[...] = dot3_nt((dense_h[...], dense_l[...]), projected_grad)[0:16, :]
        dense_grad_out[...] = dot3_nn(split(weight_pad[...]), projected_grad)[0:DENSE, :]

    weight_copies = [
        remote(
            weight_part.at[pl.ds(pl.multiple_of((1 - core) * 8, 8), 8)], weight_swap,
            weight_send.at[0], weight_recv.at[0], sibling, h,
        )
    ]
    weight_copies[0].start()

    @block
    def _():
        slot_sum[...] = scatter(16, TABLES)

    weight_copies[0].wait_recv()
    weight_swap[...] += weight_part[pl.ds(pl.multiple_of(core * 8, 8), 8), :]
    weight_at = pl.ds(pl.multiple_of(chip * 8, 8), 8)
    for other in chips:
        remote(weight_swap, weight_got.at[weight_at], weight_ssem, weight_rsem, other * 2 + core, h).start()
    weight_got[weight_at, :] = weight_swap[...]
    send_sums(1)
    block(lambda: feature_grad(0, 256))

    @block
    def _():
        slot_turned = slot_sum[...] + scatter(0, 16)
        slot_turned = (slot_turned[0:128, :] + slot_turned[128:256, :]).T
        for q in range(4):
            message[pl.ds(q, BATCH, stride=4), :] = slot_turned[q * 32 : q * 32 + 32, :]

    for other in plane:
        remote(message.at[pl.ds(other * 4, 4)], got.at[pl.ds(b * 4, 4)], slot_ssem, slot_rsem, other, h).start()
    got[pl.ds(b * 4, 4), :] = message[pl.ds(b * 4, 4), :]
    send_sums(2)
    send_sums(3)
    bulk_wait(weight_got.at[pl.ds(0, 15 * 8)], weight_rsem)
    value = weight_got[0:8, :]
    for i in range(1, 16):
        value = value + weight_got[i * 8 : i * 8 + 8, :]
    weight_at = pl.ds(pl.multiple_of(core * 8, 8), 8)
    weight_total[weight_at, :] = value
    weight_copies.append(
        remote(
            weight_total.at[weight_at], weight_total.at[weight_at], weight_send.at[1], weight_recv.at[1], sibling, h
        )
    )
    weight_copies[1].start()
    for k in range(TASKS):
        pred_out[k : k + 1, :] = pred[k : k + 1, pl.ds(pl.multiple_of(h * 128, 128), 128)]

    hand_on(0)
    hand_on(1)
    bulk_wait(got.at[pl.ds(0, (BATCH - 1) * 4)], slot_rsem)

    @block
    def _():
        high, rest = split(jnp.concatenate([got[pl.ds(q, BATCH, stride=4), :] for q in range(4)], 0).T)
        table = ids[...] // ROWS
        spreads = []
        for j in range(8):
            where = jnp.broadcast_to(table[j : j + 1, :], (ENTRY, 128)).astype(jnp.int16)
            nothing = jnp.zeros((ENTRY, 128), bf16)
            chosen = [
                jnp.where(where == t, value[j * 16 : j * 16 + 16, :], nothing)
                for value in (high, rest)
                for t in range(TABLES)
            ]
            spreads.append(jnp.concatenate(chosen, 0))
        both = dot_nt(jnp.concatenate(spreads, 1), hot_rows[...])
        table_out[...] = both[0:EMBED, :] + both[EMBED : 2 * EMBED, :]

    weight_copies[1].wait_recv()
    weight_grad_out[...] = weight_total[0:DENSE, 0:PROJ]
    hand_on(2)
    hand_on(3)
    whole = in_total.at[pl.ds(0, IN_ROWS // 2 + 16 * REST_PIECE)]
    bulk_wait(whole, last_rsem)
    head_grad_out[0:1, :] = rest_total[HEAD_AT : HEAD_AT + 1, 0:TOWER]
    head_grad_out[1:2, :] = rest_total[HEAD_AT : HEAD_AT + 1, TOWER : 2 * TOWER]
    most = in_total.at[pl.ds(0, 15 * (IN_ROWS // 32 + REST_PIECE))]
    bulk_wait(most, full_ssem)
    bulk_wait(most, piece_ssem)
    bulk_wait(whole, swap_ssem)
    bulk_wait(whole, last_ssem)
    for copy in weight_copies:
        copy.wait_send()
    bulk_wait(weight_got.at[pl.ds(0, 15 * 8)], weight_ssem)
    bulk_wait(message.at[pl.ds(0, (BATCH - 1) * 4)], slot_ssem)
    bulk_wait(rows.at[pl.ds(0, (DEVICES - 1) * 4)], row_ssem)
    bulk_wait(id_send.at[pl.ds(0, BATCH - 1)], id_ssem)
    bulk_wait(win_all.at[0, pl.ds(0, 192)], y_ssem)
    bulk_wait(win_all.at[pl.ds(0, 3), pl.ds(0, 192)], p_ssem)
    bulk_wait(win_all.at[pl.ds(0, 3), pl.ds(0, 256)], c_ssem)
    bulk_wait(wout_all.at[pl.ds(0, 3), pl.ds(0, 256)], wo_ssem)
    bulk_wait(wout_all.at[pl.ds(0, 3), pl.ds(0, 256)], woc_ssem)
    bulk_wait(cot_all.at[pl.ds(0, 3)], cot_ssem)


def write_kernel(
    table, in_total, rest_total, weight_grad, head_grad, pred, dense_grad,
    table_out, in_out, out_out, tower_out, gate_out, weight_out, head_out, pred_out, dense_out, sems,
):
    copies = [(table, table_out), (rest_total.at[OUT_AT:GATE_AT], out_out), (rest_total.at[TOWER_AT:HEAD_AT], tower_out)]
    copies += [
        (
            in_total.at[pl.ds((4 * first + q * (last - first)) * UNITS, (last - first) * UNITS)],
            in_out.at[first * UNITS : last * UNITS, q * 128 : (q + 1) * 128],
        )
        for first, last in IN_PARTS
        for q in range(4)
    ]
    copies += [
        (rest_total.at[GATE_AT + q * 16 : GATE_AT + q * 16 + 16], gate_out.at[:, q * 128 : q * 128 + 128])
        for q in range(4)
    ]
    copies += [(weight_grad, weight_out), (head_grad, head_out), (pred, pred_out), (dense_grad, dense_out)]
    copies = [pltpu.make_async_copy(source, home, sems.at[i]) for i, (source, home) in enumerate(copies)]
    for copy in copies:
        copy.start()
    for copy in copies:
        copy.wait()


def on_device(
    tables, dense, dense_weight, expert_in, expert_out, gate_weight, tower_weight, head_weight, slots, requests, pred_cot
):
    i32 = jnp.int32
    dma = pltpu.SemaphoreType.DMA
    vmem = pltpu.VMEM
    anywhere = pl.BlockSpec(memory_space=pl.ANY)
    arrays = (
        requests[0].T,
        tables.transpose(0, 2, 1).reshape(EMBED, ROWS),
        expert_in.transpose(1, 2, 0).reshape(EXPERTS * UNITS, WIDTH),
        expert_out.reshape(EXPERTS * UNITS, OUT),
        pred_cot.T,
        slots.T,
        dense.T,
        dense_weight,
        gate_weight.transpose(0, 2, 1).reshape(TASKS * EXPERTS, WIDTH),
        tower_weight.transpose(0, 2, 1).reshape(TASKS * TOWER, OUT),
        head_weight,
    )
    shape = lambda *dims: jax.ShapeDtypeStruct(dims, f32)
    units = HIDDEN * 512, EXAMPLES
    outputs = EXPERTS, OUT, EXAMPLES
    results = pl.pallas_call(
        model_kernel,
        out_shape=[
            vmem((TASKS, 128), f32), vmem((DENSE, EXAMPLES), f32), vmem((EMBED, ROWS), f32), vmem((IN_ROWS, 128), f32),
            vmem((REST_ROWS, 128), f32), vmem((DENSE, PROJ), f32), vmem((TASKS, TOWER), f32),
        ],
        in_specs=[anywhere] * 11,
        out_specs=[VMEM] * 7,
        scratch_shapes=[
            vmem((32, 128), i32), vmem((EMBED, ROWS), f32), vmem((TASKS, 128), f32), vmem((TABLES, EXAMPLES), i32),
            vmem((DENSE, EXAMPLES), f32), vmem((DENSE, PROJ), f32), vmem((16, WIDTH), f32), vmem((128, OUT), f32),
            vmem((TASKS, TOWER), f32),
            vmem((128, 128), i32), vmem((32, 128), i32), vmem((32, 128), i32), vmem((8, 128), i32), vmem((128, 128), f32),
            vmem((512, 128), f32), vmem((2 * EMBED, ROWS), bf16),
            vmem((HIDDEN, 512, WIDTH), f32), vmem((HIDDEN, 512, OUT), f32), vmem((HIDDEN, TASKS, 128), f32),
            vmem((2048, WIDTH), bf16), vmem((2048, WIDTH), bf16), vmem((2048, OUT), bf16), vmem((2048, OUT), bf16),
            vmem((16, WIDTH), bf16), vmem((16, WIDTH), bf16), vmem((128, OUT), bf16), vmem((128, OUT), bf16),
            vmem((128, EXAMPLES), bf16), vmem((128, EXAMPLES), bf16),
            vmem((256, 512), bf16), vmem((WIDTH, EXAMPLES), bf16), vmem((WIDTH, EXAMPLES), bf16),
            vmem((128, EXAMPLES), f32), vmem((128, 128), f32), vmem((128, 128), f32),
            vmem(units, bf16), vmem(units, bf16), vmem(units, f32), vmem(units, bf16), vmem(units, bf16),
            vmem(outputs, f32), vmem(outputs, f32), vmem(outputs, bf16), vmem(outputs, bf16),
            vmem((16, EXAMPLES), f32), vmem((16, EXAMPLES), f32),
            vmem((TASKS, OUT, EXAMPLES), f32), vmem((TASKS, OUT, EXAMPLES), f32), vmem((TASKS, EXAMPLES), f32),
            vmem((128, EXAMPLES), f32), vmem((128, EXAMPLES), f32), vmem((16, EXAMPLES), f32),
            vmem((16, EXAMPLES), bf16), vmem((16, EXAMPLES), bf16),
            vmem((WIDTH, EXAMPLES), f32), vmem((256, 128), f32),
            vmem((IN_ROWS, 128), f32), vmem((REST_ROWS, 128), f32), vmem((IN_ROWS // 2, 128), f32),
            vmem((16 * REST_PIECE, 128), f32), vmem((IN_ROWS // 2, 128), f32), vmem((16 * REST_PIECE, 128), f32),
            vmem((128, 128), f32), vmem((128, 128), f32), vmem((16, 128), f32), vmem((8, 128), f32),
            vmem((128, 128), f32), vmem((16, 128), f32), vmem((ROWS, ROWS), bf16),
            vmem((128, TABLES * EXAMPLES), bf16),
            dma((11,)), dma, dma((3,)), dma, dma((3,)), dma, dma((3,)), dma, dma((3,)), dma, dma, dma, dma,
            dma, dma, dma, dma, dma, dma, dma, dma, dma((2,)), dma((2,)),
            dma, dma((4,)), dma, dma((4,)), dma, dma((4,)), dma, dma,
        ],
        compiler_params=pltpu.CompilerParams(vmem_limit_bytes=LIMIT, collective_id=0, has_side_effects=True),
        name="model",
    )(*arrays)
    results = [pltpu.with_memory_space_constraint(result, pltpu.VMEM) for result in results]
    pred, dense_grad, table_grad, in_total, rest_total, weight_grad, head_grad = results
    table_grad, in_grad, out_grad, tower_grad, gate_grad, weight_grad, head_grad, pred, dense_grad = pl.pallas_call(
        write_kernel,
        out_shape=[
            shape(EMBED, ROWS), shape(512, WIDTH), shape(512, OUT), shape(TASKS * TOWER, OUT),
            shape(TASKS * EXPERTS, WIDTH), shape(DENSE, PROJ), shape(TASKS, TOWER), shape(TASKS, 128),
            shape(DENSE, EXAMPLES),
        ],
        in_specs=[anywhere] * 7,
        out_specs=[anywhere] * 9,
        scratch_shapes=[dma((23,))],
        compiler_params=pltpu.CompilerParams(vmem_limit_bytes=LIMIT),
        name="write",
    )(table_grad, in_total, rest_total, weight_grad, head_grad, pred, dense_grad)
    return (
        pred.T,
        dense_grad.T,
        table_grad.reshape(TABLES, ENTRY, ROWS).transpose(0, 2, 1),
        weight_grad,
        in_grad.reshape(EXPERTS, UNITS, WIDTH).transpose(2, 0, 1),
        out_grad.reshape(EXPERTS, UNITS, OUT),
        gate_grad.reshape(TASKS, EXPERTS, WIDTH).transpose(0, 2, 1),
        tower_grad.reshape(TASKS, TOWER, OUT).transpose(0, 2, 1),
        head_grad,
    )


def solution(mesh):
    placed = (
        P(None, ("batch", "hidden"), None),
        P("batch", None),
        P(),
        P(None, None, "hidden"),
        P(None, "hidden", None),
        P(),
        P(),
        P(),
        P("batch", None),
        P("batch", None, None),
        P(("batch", "hidden"), None),
    )
    return jax.shard_map(
        on_device,
        mesh=mesh,
        in_specs=placed,
        out_specs=(
            P(("batch", "hidden"), None),
            P("batch", None),
            P(None, ("batch", "hidden"), None),
            P(),
            P(None, None, "hidden"),
            P(None, "hidden", None),
            P(),
            P(),
            P(),
        ),
        check_vma=False,
    )
```

profile of v0, /device:TPU:1, one launch (start us, length us, event | category | flops | bytes accessed | tf_op | source)
XLA Modules:
  0.0 62.5 jit_solution(9797393357356115383)
XLA Ops:
  0.6 59.9 %model.1 = (f32[2,128]{1,0:T(2,128)S(1)}, f32[13,512]{1,0:T(8,128)S(1)}, f32[416,1024]{1,0:T(8,128)S(1)}, f32[2048,128]{1,0:T(8,128)S(1)}, f32[768,128]{1,0:T(8,...) custom-call(s32[32,128]{1,0:T(8,128)} %bitcast.41, f32[416,1024]{1,0:T(8,128)} %bitcast.34, f32[512,512]{1,0:T(8,128)} %bitcast.35, ...), custom_call_target="tpu_custom_call" | custom-call | tf_op jit(solution)/shard_map/model/pallas_call | solution.py:669
  60.5 1.9 %write.1 = (f32[416,1024]{1,0:T(8,128)}, f32[512,512]{1,0:T(8,128)}, f32[512,128]{1,0:T(8,128)}, f32[128,128]{1,0:T(8,128)}, f32[16,512]{1,0:T(8,128)}, /*index=...) custom-call(f32[416,1024]{1,0:T(8,128)S(1)} %get-tuple-element.25.table, ...), custom_call_target="tpu_custom_call" | custom-call | tf_op jit(solution)/shard_map/write/pallas_call | solution.py:710
where the time goes:
time: 62.7 us; the launch traced here: 62.5 us
  Pallas kernels  61.7 us (98%)
  between operations  0.81 us (1%)
    pallas_call x1, Pallas kernels, on_device(): pl.pallas_call(model_kernel, out_shape=[vmem((TASKS, 128), f32), vmem((DE...  59.9 us
    pallas_call x1, Pallas kernels, on_device(): pl.pallas_call(write_kernel, out_shape=[shape(EMBED, ROWS), shape(512, WI...  1.86 us

commit v1 on v0

--- a/solution.py
+++ b/solution.py
@@ -54,7 +54,9 @@
 
 def dot3_nt(a, b):
     (ah, al), (bh, bl) = a, b
-    return dot_nt(jnp.concatenate([ah, al, ah], 1), jnp.concatenate([bh, bh, bl], 1))
+    count = ah.shape[0]
+    both = dot_nt(jnp.concatenate([ah, al], 0), bh)
+    return both[0:count, :] + both[count : 2 * count, :] + dot_nt(ah, bl)
 
 
 def sigmoid(value):
@@ -398,9 +400,7 @@
     def first_layer_grad(first, last):
         count = (last - first) * UNITS
         at = pl.ds(pl.multiple_of(h * 512 + first * UNITS, UNITS), count)
-        ig, ig_low = ig_h[at, :], ig_l[at, :]
-        in_grad = dot_nt(jnp.concatenate([ig, ig_low], 0), feat_h[...])
-        in_grad = in_grad[0:count, :] + in_grad[count : 2 * count, :] + dot_nt(ig, feat_l[...])
+        in_grad = dot3_nt((ig_h[at, :], ig_l[at, :]), (feat_h[...], feat_l[...]))
         for q in range(4):
             start = 4 * first * UNITS + q * count
             in_sums[start : start + count, :] = in_grad[:, q * 128 : (q + 1) * 128]

time: 62.7 us -> 62.3 us (level)
  no operation moved by 1% of the time
where the time goes in v1:
time: 62.3 us; the launch traced here: 62.1 us
  Pallas kernels  61.3 us (98%)
  between operations  0.81 us (1%)
    pallas_call x1, Pallas kernels, on_device(): pl.pallas_call(model_kernel, out_shape=[vmem((TASKS, 128), f32), vmem((DE...  59.5 us
    pallas_call x1, Pallas kernels, on_device(): pl.pallas_call(write_kernel, out_shape=[shape(EMBED, ROWS), shape(512, WI...  1.86 us

profile of v1, /device:TPU:1, one launch (start us, length us, event | category | flops | bytes accessed | tf_op | source)
XLA Modules:
  0.0 62.1 jit_solution(7566764900194681035)
XLA Ops:
  0.6 59.5 %model.1 = (f32[2,128]{1,0:T(2,128)S(1)}, f32[13,512]{1,0:T(8,128)S(1)}, f32[416,1024]{1,0:T(8,128)S(1)}, f32[2048,128]{1,0:T(8,128)S(1)}, f32[768,128]{1,0:T(8,...) custom-call(s32[32,128]{1,0:T(8,128)} %bitcast.41, f32[416,1024]{1,0:T(8,128)} %bitcast.34, f32[512,512]{1,0:T(8,128)} %bitcast.35, ...), custom_call_target="tpu_custom_call" | custom-call | tf_op jit(solution)/shard_map/model/pallas_call | solution.py:669
  60.1 1.9 %write.1 = (f32[416,1024]{1,0:T(8,128)}, f32[512,512]{1,0:T(8,128)}, f32[512,128]{1,0:T(8,128)}, f32[128,128]{1,0:T(8,128)}, f32[16,512]{1,0:T(8,128)}, /*index=...) custom-call(f32[416,1024]{1,0:T(8,128)S(1)} %get-tuple-element.25.table, ...), custom_call_target="tpu_custom_call" | custom-call | tf_op jit(solution)/shard_map/write/pallas_call | solution.py:710

commit v2 on v1

--- a/solution.py
+++ b/solution.py
@@ -347,8 +347,7 @@
             for ref in refs
         )
 
-    @block
-    def _():
+    def second_layer():
         mixed[...] = jnp.zeros_like(mixed)
         for s in range(HIDDEN):
             at = slice(s * 512, s * 512 + 512)
@@ -359,8 +358,7 @@
             for k in range(TASKS):
                 mixed[k] = mixed[k] + gates[k * 8 + e : k * 8 + e + 1, :] * outputs
 
-    @block
-    def _():
+    def tower_pass():
         head_turned = head_pad[...].T
         scores[...] = jnp.zeros_like(scores)
         for k in range(TASKS):
@@ -376,6 +374,11 @@
             pre_grad = score * column * tower_slope
             pre_grads[at, :] = pre_grad
             mixed_grad[k] = dot3_tn((tower_h[at, :], tower_l[at, :]), split(pre_grad))
+
+    @block
+    def _():
+        second_layer()
+        tower_pass()
 
     def expert_grads(first, last):
         for e in range(first, last):
@@ -481,10 +484,6 @@
         for q in range(4):
             rest_sums[GATE_AT + q * 16 : GATE_AT + q * 16 + 16, :] = gate_grad[:, q * 128 : (q + 1) * 128]
 
-    send_pieces(2)
-
-    @block
-    def _():
         for e in range(EXPERTS):
             at = units_of(h, e)
             rest_sums[OUT_AT + e * UNITS : OUT_AT + (e + 1) * UNITS, :] = dot3_nt(
@@ -492,6 +491,7 @@
             )
 
     swap(3)
+    send_pieces(2)
 
     def feature_grad(low, high):
         at = slice(low, high)
@@ -541,10 +541,10 @@
         remote(weight_swap, weight_got.at[weight_at], weight_ssem, weight_rsem, other * 2 + core, h).start()
     weight_got[weight_at, :] = weight_swap[...]
     send_sums(1)
-    block(lambda: feature_grad(0, 256))
-
-    @block
-    def _():
+
+    @block
+    def _():
+        feature_grad(0, 256)
         slot_turned = slot_sum[...] + scatter(0, 16)
         slot_turned = (slot_turned[0:128, :] + slot_turned[128:256, :]).T
         for q in range(4):

time: 62.3 us -> 62.2 us (level)
  no operation moved by 1% of the time
where the time goes in v2:
time: 62.2 us; the launch traced here: 62 us
  Pallas kernels  61.2 us (98%)
  between operations  0.81 us (1%)
    pallas_call x1, Pallas kernels, on_device(): pl.pallas_call(model_kernel, out_shape=[vmem((TASKS, 128), f32), vmem((DE...  59.3 us
    pallas_call x1, Pallas kernels, on_device(): pl.pallas_call(write_kernel, out_shape=[shape(EMBED, ROWS), shape(512, WI...  1.86 us

profile of v2, /device:TPU:1, one launch (start us, length us, event | category | flops | bytes accessed | tf_op | source)
XLA Modules:
  0.0 62.0 jit_solution(8822636463744218356)
XLA Ops:
  0.6 59.3 %model.1 = (f32[2,128]{1,0:T(2,128)S(1)}, f32[13,512]{1,0:T(8,128)S(1)}, f32[416,1024]{1,0:T(8,128)S(1)}, f32[2048,128]{1,0:T(8,128)S(1)}, f32[768,128]{1,0:T(8,...) custom-call(s32[32,128]{1,0:T(8,128)} %bitcast.41, f32[416,1024]{1,0:T(8,128)} %bitcast.34, f32[512,512]{1,0:T(8,128)} %bitcast.35, ...), custom_call_target="tpu_custom_call" | custom-call | tf_op jit(solution)/shard_map/model/pallas_call | solution.py:669
  59.9 1.9 %write.1 = (f32[416,1024]{1,0:T(8,128)}, f32[512,512]{1,0:T(8,128)}, f32[512,128]{1,0:T(8,128)}, f32[128,128]{1,0:T(8,128)}, f32[16,512]{1,0:T(8,128)}, /*index=...) custom-call(f32[416,1024]{1,0:T(8,128)S(1)} %get-tuple-element.25.table, ...), custom_call_target="tpu_custom_call" | custom-call | tf_op jit(solution)/shard_map/write/pallas_call | solution.py:710

commit v3 on v2

--- a/solution.py
+++ b/solution.py
@@ -125,9 +125,9 @@
     towers, pre_grads, scores, lgh, lgl, fg, slot_sum,
     in_sums, rest_sums, in_swap, rest_swap, in_pieces, rest_pieces,
     message, got, weight_part, weight_swap, weight_got, weight_total, hot_rows, hot_slots,
-    local_sem, y_ssem, y_rsem, p_ssem, p_rsem, c_ssem, c_rsem, wo_ssem, wo_rsem, woc_ssem, woc_rsem, cot_ssem, cot_rsem,
-    id_ssem, id_rsem, row_ssem, row_rsem, slot_ssem, slot_rsem, weight_ssem, weight_rsem, weight_send, weight_recv,
-    swap_ssem, swap_rsem, piece_ssem, piece_rsem, full_ssem, full_rsem, last_ssem, last_rsem,
+    local_sem, y_rsem, p_rsem, c_rsem, wo_rsem, woc_rsem, cot_ssem, cot_rsem,
+    id_rsem, row_rsem, slot_rsem, weight_rsem, weight_send, weight_recv, swap_rsem, piece_rsem, full_rsem, last_rsem,
+    small_ssem, sum_ssem, side_ssem, piece_ssem, full_ssem,
 ):
     b, h = lax.axis_index("batch"), lax.axis_index("hidden")
     core, x, z, chip = lax.rem(b, 2), lax.rem(b // 2, 4), b // 8, b // 2
@@ -171,7 +171,7 @@
     pl.semaphore_wait(barrier, BATCH - 1 + HIDDEN - 1)
 
     for other in plane:
-        remote(id_send.at[pl.ds(other, 1)], id_recv.at[pl.ds(b, 1)], id_ssem, id_rsem, other, h).start()
+        remote(id_send.at[pl.ds(other, 1)], id_recv.at[pl.ds(b, 1)], small_ssem, id_rsem, other, h).start()
     spots = (
         pl.ds(pl.multiple_of(core * 128 + x * 32, 32), 32),
         pl.ds(pl.multiple_of(256 + core * 128 + z * 32, 32), 32),
@@ -181,7 +181,7 @@
     source_of = [lax.rem(h - i + HIDDEN, HIDDEN) for i in range(HIDDEN)]
     for i in order:
         for spot in spots:
-            remote(win.at[spot], win_all.at[h, spot], y_ssem, y_rsem.at[i - 1], b, hs[i]).start()
+            remote(win.at[spot], win_all.at[h, spot], side_ssem, y_rsem.at[i - 1], b, hs[i]).start()
 
     def spread(i):
         source = source_of[i]
@@ -189,19 +189,19 @@
         for j in (2, 1, 3):
             for spot, other in ((spots[0], z * 8 + xs[j] + core), (spots[1], zs[j] + x * 2 + core)):
                 piece = win_all.at[source, spot]
-                remote(piece, piece, p_ssem, p_rsem.at[i - 1], other, h).start()
+                remote(piece, piece, side_ssem, p_rsem.at[i - 1], other, h).start()
 
     def to_core(i):
         source = source_of[i]
         bulk_wait(win_all.at[source, pl.ds(0, 192)], p_rsem.at[i - 1])
         for span in spans:
             piece = win_all.at[source, span]
-            remote(piece, piece, c_ssem, c_rsem.at[i - 1], sibling, h).start()
+            remote(piece, piece, side_ssem, c_rsem.at[i - 1], sibling, h).start()
 
     def out_to_core(i):
         bulk_wait(wout_all.at[source_of[i], half], wo_rsem.at[i - 1])
         piece = wout_all.at[source_of[i], half]
-        remote(piece, piece, woc_ssem, woc_rsem, sibling, h).start()
+        remote(piece, piece, side_ssem, woc_rsem, sibling, h).start()
 
     tab_copy.wait()
 
@@ -238,7 +238,7 @@
     mine = pl.ds(me * 4, 4)
     for dz, dx, dc, dy in EVERYWHERE:
         group = zs[dz] + xs[dx] + cores[dc]
-        remote(row_send.at[pl.ds(group * 4, 4)], rows.at[mine], row_ssem, row_rsem, group, hs[dy]).start()
+        remote(row_send.at[pl.ds(group * 4, 4)], rows.at[mine], small_ssem, row_rsem, group, hs[dy]).start()
     rows[mine, :] = row_send[pl.ds(b * 4, 4), :]
     for i in order:
         spread(i)
@@ -248,7 +248,7 @@
     for i in order:
         remote(cot, cot_all.at[h], cot_ssem, cot_rsem, b, hs[i]).start()
         piece = wout_all.at[h, half]
-        remote(piece, piece, wo_ssem, wo_rsem.at[i - 1], b, hs[i]).start()
+        remote(piece, piece, side_ssem, wo_rsem.at[i - 1], b, hs[i]).start()
     win_copy.wait()
 
     @block
@@ -375,11 +375,6 @@
             pre_grads[at, :] = pre_grad
             mixed_grad[k] = dot3_tn((tower_h[at, :], tower_l[at, :]), split(pre_grad))
 
-    @block
-    def _():
-        second_layer()
-        tower_pass()
-
     def expert_grads(first, last):
         for e in range(first, last):
             outputs = eo[e]
@@ -419,7 +414,7 @@
         sums, swapped, _, _, piece = parts[n]
         half_rows = 16 * piece
         theirs = sums.at[pl.ds(pl.multiple_of((1 - core) * half_rows, 8), half_rows)]
-        remote(theirs, swapped, swap_ssem, swap_rsem.at[n], sibling, h).start()
+        remote(theirs, swapped, sum_ssem, swap_rsem.at[n], sibling, h).start()
 
     def send_pieces(n):
         sums, swapped, pieces, _, piece = parts[n]
@@ -450,12 +445,15 @@
         _, _, _, total, piece = parts[n]
         bulk_wait(total.at[pl.ds(0, 15 * piece)], full_rsem.at[n])
         ours = total.at[pl.ds(pl.multiple_of(core * 16 * piece, 8), 16 * piece)]
-        remote(ours, ours, last_ssem, last_rsem, sibling, h).start()
+        remote(ours, ours, sum_ssem, last_rsem, sibling, h).start()
 
     for n, (first, last) in enumerate(IN_PARTS):
 
         @block
         def _():
+            if n == 0:
+                second_layer()
+                tower_pass()
             expert_grads(first, last)
             first_layer_grad(first, last)
 
@@ -538,7 +536,7 @@
     weight_swap[...] += weight_part[pl.ds(pl.multiple_of(core * 8, 8), 8), :]
     weight_at = pl.ds(pl.multiple_of(chip * 8, 8), 8)
     for other in chips:
-        remote(weight_swap, weight_got.at[weight_at], weight_ssem, weight_rsem, other * 2 + core, h).start()
+        remote(weight_swap, weight_got.at[weight_at], small_ssem, weight_rsem, other * 2 + core, h).start()
     weight_got[weight_at, :] = weight_swap[...]
     send_sums(1)
 
@@ -551,7 +549,7 @@
             message[pl.ds(q, BATCH, stride=4), :] = slot_turned[q * 32 : q * 32 + 32, :]
 
     for other in plane:
-        remote(message.at[pl.ds(other * 4, 4)], got.at[pl.ds(b * 4, 4)], slot_ssem, slot_rsem, other, h).start()
+        remote(message.at[pl.ds(other * 4, 4)], got.at[pl.ds(b * 4, 4)], small_ssem, slot_rsem, other, h).start()
     got[pl.ds(b * 4, 4), :] = message[pl.ds(b * 4, 4), :]
     send_sums(2)
     send_sums(3)
@@ -599,23 +597,15 @@
     bulk_wait(whole, last_rsem)
     head_grad_out[0:1, :] = rest_total[HEAD_AT : HEAD_AT + 1, 0:TOWER]
     head_grad_out[1:2, :] = rest_total[HEAD_AT : HEAD_AT + 1, TOWER : 2 * TOWER]
-    most = in_total.at[pl.ds(0, 15 * (IN_ROWS // 32 + REST_PIECE))]
-    bulk_wait(most, full_ssem)
-    bulk_wait(most, piece_ssem)
-    bulk_wait(whole, swap_ssem)
-    bulk_wait(whole, last_ssem)
     for copy in weight_copies:
         copy.wait_send()
-    bulk_wait(weight_got.at[pl.ds(0, 15 * 8)], weight_ssem)
-    bulk_wait(message.at[pl.ds(0, (BATCH - 1) * 4)], slot_ssem)
-    bulk_wait(rows.at[pl.ds(0, (DEVICES - 1) * 4)], row_ssem)
-    bulk_wait(id_send.at[pl.ds(0, BATCH - 1)], id_ssem)
-    bulk_wait(win_all.at[0, pl.ds(0, 192)], y_ssem)
-    bulk_wait(win_all.at[pl.ds(0, 3), pl.ds(0, 192)], p_ssem)
-    bulk_wait(win_all.at[pl.ds(0, 3), pl.ds(0, 256)], c_ssem)
-    bulk_wait(wout_all.at[pl.ds(0, 3), pl.ds(0, 256)], wo_ssem)
-    bulk_wait(wout_all.at[pl.ds(0, 3), pl.ds(0, 256)], woc_ssem)
     bulk_wait(cot_all.at[pl.ds(0, 3)], cot_ssem)
+    bulk_wait(slope.at[pl.ds(0, 2 * 16 * (IN_ROWS // 32 + REST_PIECE) // 4)], sum_ssem)
+    most = in_total.at[pl.ds(0, 15 * (IN_ROWS // 32 + REST_PIECE))]
+    bulk_wait(most, piece_ssem)
+    bulk_wait(most, full_ssem)
+    bulk_wait(in_total.at[pl.ds(0, BATCH - 1 + (DEVICES - 1) * 4 + (BATCH - 1) * 4 + 15 * 8)], small_ssem)
+    bulk_wait(slope.at[pl.ds(0, 192 + 576 + 768 + 2 * 192)], side_ssem)
 
 
 def write_kernel(
@@ -698,9 +688,9 @@
             vmem((128, 128), f32), vmem((128, 128), f32), vmem((16, 128), f32), vmem((8, 128), f32),
             vmem((128, 128), f32), vmem((16, 128), f32), vmem((ROWS, ROWS), bf16),
             vmem((128, TABLES * EXAMPLES), bf16),
-            dma((11,)), dma, dma((3,)), dma, dma((3,)), dma, dma((3,)), dma, dma((3,)), dma, dma, dma, dma,
-            dma, dma, dma, dma, dma, dma, dma, dma, dma((2,)), dma((2,)),
-            dma, dma((4,)), dma, dma((4,)), dma, dma((4,)), dma, dma,
+            dma((11,)), dma((3,)), dma((3,)), dma((3,)), dma((3,)), dma, dma, dma,
+            dma, dma, dma, dma, dma((2,)), dma((2,)), dma((4,)), dma((4,)), dma((4,)), dma,
+            dma, dma, dma, dma, dma,
         ],
         compiler_params=pltpu.CompilerParams(vmem_limit_bytes=LIMIT, collective_id=0, has_side_effects=True),
         name="model",

time: 62.2 us -> 62.1 us (level)
  no operation moved by 1% of the time
where the time goes in v3:
time: 62.1 us; the launch traced here: 61.9 us
  Pallas kernels  61.1 us (98%)
  between operations  0.81 us (1%)
    pallas_call x1, Pallas kernels, on_device(): pl.pallas_call(model_kernel, out_shape=[vmem((TASKS, 128), f32), vmem((DE...  59.2 us
    pallas_call x1, Pallas kernels, on_device(): pl.pallas_call(write_kernel, out_shape=[shape(EMBED, ROWS), shape(512, WI...  1.86 us

profile of v3, /device:TPU:1, one launch (start us, length us, event | category | flops | bytes accessed | tf_op | source)
XLA Modules:
  0.0 61.9 jit_solution(8730334482825753248)
XLA Ops:
  0.6 59.2 %model.1 = (f32[2,128]{1,0:T(2,128)S(1)}, f32[13,512]{1,0:T(8,128)S(1)}, f32[416,1024]{1,0:T(8,128)S(1)}, f32[2048,128]{1,0:T(8,128)S(1)}, f32[768,128]{1,0:T(8,...) custom-call(s32[32,128]{1,0:T(8,128)} %bitcast.41, f32[416,1024]{1,0:T(8,128)} %bitcast.34, f32[512,512]{1,0:T(8,128)} %bitcast.35, ...), custom_call_target="tpu_custom_call" | custom-call | tf_op jit(solution)/shard_map/model/pallas_call | solution.py:659
  59.9 1.9 %write.1 = (f32[416,1024]{1,0:T(8,128)}, f32[512,512]{1,0:T(8,128)}, f32[512,128]{1,0:T(8,128)}, f32[128,128]{1,0:T(8,128)}, f32[16,512]{1,0:T(8,128)}, /*index=...) custom-call(f32[416,1024]{1,0:T(8,128)S(1)} %get-tuple-element.25.table, ...), custom_call_target="tpu_custom_call" | custom-call | tf_op jit(solution)/shard_map/write/pallas_call | solution.py:700

commit v4 on v3

--- a/solution.py
+++ b/solution.py
@@ -375,6 +375,11 @@
             pre_grads[at, :] = pre_grad
             mixed_grad[k] = dot3_tn((tower_h[at, :], tower_l[at, :]), split(pre_grad))
 
+    @block
+    def _():
+        second_layer()
+        tower_pass()
+
     def expert_grads(first, last):
         for e in range(first, last):
             outputs = eo[e]
@@ -451,9 +456,6 @@
 
         @block
         def _():
-            if n == 0:
-                second_layer()
-                tower_pass()
             expert_grads(first, last)
             first_layer_grad(first, last)
 

time: 62.1 us -> 62.1 us (level)
  no operation moved by 1% of the time
where the time goes in v4:
time: 62.1 us; the launch traced here: 61.9 us
  Pallas kernels  61.1 us (98%)
  between operations  0.81 us (1%)
    pallas_call x1, Pallas kernels, on_device(): pl.pallas_call(model_kernel, out_shape=[vmem((TASKS, 128), f32), vmem((DE...  59.2 us
    pallas_call x1, Pallas kernels, on_device(): pl.pallas_call(write_kernel, out_shape=[shape(EMBED, ROWS), shape(512, WI...  1.86 us

profile of v4, /device:TPU:1, one launch (start us, length us, event | category | flops | bytes accessed | tf_op | source)
XLA Modules:
  0.0 61.9 jit_solution(8730334482825753248)
XLA Ops:
  0.6 59.2 %model.1 = (f32[2,128]{1,0:T(2,128)S(1)}, f32[13,512]{1,0:T(8,128)S(1)}, f32[416,1024]{1,0:T(8,128)S(1)}, f32[2048,128]{1,0:T(8,128)S(1)}, f32[768,128]{1,0:T(8,...) custom-call(s32[32,128]{1,0:T(8,128)} %bitcast.41, f32[416,1024]{1,0:T(8,128)} %bitcast.34, f32[512,512]{1,0:T(8,128)} %bitcast.35, ...), custom_call_target="tpu_custom_call" | custom-call | tf_op jit(solution)/shard_map/model/pallas_call | solution.py:661
  59.9 1.9 %write.1 = (f32[416,1024]{1,0:T(8,128)}, f32[512,512]{1,0:T(8,128)}, f32[512,128]{1,0:T(8,128)}, f32[128,128]{1,0:T(8,128)}, f32[16,512]{1,0:T(8,128)}, /*index=...) custom-call(f32[416,1024]{1,0:T(8,128)S(1)} %get-tuple-element.25.table, ...), custom_call_target="tpu_custom_call" | custom-call | tf_op jit(solution)/shard_map/write/pallas_call | solution.py:702
